TPU v7x, 256 devices: a whole 4x4x8 slice. The times are simulated.
256 devices in a mesh: row: 8 (over y, x_lo), col: 16 (over z, core), frame: 2 (over x_hi).
Axes of the slice: x: 4 (x_hi: 2, x_lo: 2; x = x_hi * 2 + x_lo), y: 4, z: 8, core: 2. Of those that a mesh axis runs over, the one named last changes fastest.
Arguments:
- tokens: bfloat16 [131072, 1536], P(('frame', 'row', 'col')), parts along dimension 0, may hold values from -6 to 6
- project_weight: bfloat16 [1536, 384], replicated, may hold values from -0.15625 to 0.15625
- project_bias: float32 [384], replicated, may hold values from -3 to 3
- inner_weight: bfloat16 [3, 3, 384, 384], replicated, may hold values from -0.109375 to 0.109375
- inner_bias: float32 [384], replicated, may hold values from -3 to 3
- outer_weight: bfloat16 [3, 3, 384, 384], replicated, may hold values from -0.109375 to 0.109375
- outer_bias: float32 [384], replicated, may hold values from -3 to 3
- cotangent: bfloat16 [512, 256, 384], P(('frame', 'row'), 'col'), parts along dimension 0, may hold values from -6 to 6
Outputs:
- refined: bfloat16 [512, 256, 384], P(('frame', 'row'), 'col'), parts along dimension 0
- grad_tokens: bfloat16 [131072, 1536], P(('frame', 'row', 'col')), parts along dimension 0
- grad_project: float32 [3072, 384], P(('frame', 'row'), 'col'), parts along dimension 0
- grad_inner: float32 [6, 3, 384, 384], P('frame', None, 'row', 'col'), parts along dimension 0
- grad_outer: float32 [6, 3, 384, 384], P('frame', None, 'row', 'col'), parts along dimension 0
There are 2 independent parts, one for each index of `frame`. A program takes and returns all parts, laid end to end along the dimension named above; an argument that names none is the same for every part. Nothing has to cross between parts.
All inputs are finite; a program needn't handle non-finite values.
Results may differ from a plain program's by a relative error of at most 0.027.
Values may be sent and summed in bfloat16 or wider, within the bound.
A program may use at most 128 MiB of HBM per device.

v0:
```python
import math

import jax
import jax.numpy as jnp
from jax import lax
from jax.sharding import PartitionSpec as P

VIT_DIM = 1536
JOIN_DIM = 384
TILE_ROWS = 32
TILE_COLS = 16
TOK_DEV = 512


def with_halo(block, sides, width):
    for axis, dim in sides:
        count = lax.axis_size(axis)
        forward = [(i, i + 1) for i in range(count - 1)]
        backward = [(target, source) for source, target in forward]
        low = lax.ppermute(
            lax.slice_in_dim(block, block.shape[dim] - width, None, axis=dim), axis, forward
        )
        high = lax.ppermute(lax.slice_in_dim(block, 0, width, axis=dim), axis, backward)
        block = jnp.concatenate([low, block, high], axis=dim)
    return block


def silu_slope(value):
    sigma = jax.nn.sigmoid(value)
    return sigma * (1.0 + value * (1.0 - sigma))


def tile_margin(field):
    return with_halo(field, (("row", 0), ("col", 1)), 1)


def conv_apply(padded, kernel):
    rows_here = padded.shape[0] - 2
    cols_here = padded.shape[1] - 2
    chans = padded.shape[2]
    total = jnp.zeros((rows_here * cols_here, kernel.shape[3]), jnp.float32)
    for top in range(3):
        for left in range(3):
            window = padded[top : top + rows_here, left : left + cols_here].reshape(
                rows_here * cols_here, chans
            )
            total = total + jnp.dot(window, kernel[top, left], preferred_element_type=jnp.float32)
    return total.reshape(rows_here, cols_here, kernel.shape[3])


def conv_transpose(padded, kernel):
    rows_here = padded.shape[0] - 2
    cols_here = padded.shape[1] - 2
    chans = padded.shape[2]
    total = jnp.zeros((rows_here * cols_here, kernel.shape[2]), jnp.float32)
    for top in range(3):
        for left in range(3):
            window = padded[2 - top : 2 - top + rows_here, 2 - left : 2 - left + cols_here].reshape(
                rows_here * cols_here, chans
            )
            total = total + jnp.dot(window, kernel[top, left].T, preferred_element_type=jnp.float32)
    return total.reshape(rows_here, cols_here, kernel.shape[2])


def weight_grad(padded, upstream):
    rows_here = upstream.shape[0]
    cols_here = upstream.shape[1]
    chans = padded.shape[2]
    flat_up = upstream.reshape(rows_here * cols_here, upstream.shape[2])
    blocks = []
    for top in range(3):
        for left in range(3):
            window = padded[top : top + rows_here, left : left + cols_here].reshape(
                rows_here * cols_here, chans
            )
            blocks.append(
                lax.dot_general(
                    window, flat_up, (((0,), (0,)), ((), ())), preferred_element_type=jnp.float32
                )
            )
    return jnp.stack(blocks).reshape(3, 3, chans, upstream.shape[2])


def refine(feature, cotangent, inner_weight, inner_bias, outer_weight, outer_bias, margin):
    feature_wide = feature.astype(jnp.float32)
    activated = jax.nn.silu(feature_wide).astype(jnp.bfloat16)
    activated_rim = margin(activated)
    pre_hidden = conv_apply(activated_rim, inner_weight) + inner_bias
    hidden = jax.nn.silu(pre_hidden).astype(jnp.bfloat16)
    hidden_rim = margin(hidden)
    refined = (feature_wide + conv_apply(hidden_rim, outer_weight) + outer_bias).astype(
        jnp.bfloat16
    )
    grad_outer = weight_grad(hidden_rim, cotangent)
    back_hidden = (conv_transpose(margin(cotangent), outer_weight) * silu_slope(pre_hidden)).astype(
        jnp.bfloat16
    )
    grad_inner = weight_grad(activated_rim, back_hidden)
    back_feature = (
        cotangent.astype(jnp.float32)
        + conv_transpose(margin(back_hidden), inner_weight) * silu_slope(feature_wide)
    ).astype(jnp.bfloat16)
    return (refined, back_feature, grad_inner, grad_outer)


def project(field, project_weight, project_bias):
    flat = field.reshape(-1, field.shape[2])
    mapped = (
        jnp.dot(flat, project_weight, preferred_element_type=jnp.float32) + project_bias
    ).astype(jnp.bfloat16)
    return mapped.reshape(field.shape[0], field.shape[1], project_weight.shape[1])


def shards(
    tokens,
    project_weight,
    project_bias,
    inner_weight,
    inner_bias,
    outer_weight,
    outer_bias,
    cotangent,
):
    columns = lax.axis_size("col")
    strip_rows = TILE_ROWS // columns
    width_all = TILE_COLS * columns
    scale = 1.0 / math.sqrt(TILE_ROWS * lax.axis_size("row") * width_all)
    strips = tokens.reshape(strip_rows, width_all, VIT_DIM)
    feature = lax.all_to_all(
        project(strips, project_weight, project_bias),
        "col",
        split_axis=1,
        concat_axis=0,
        tiled=True,
    )
    refined, back_feature, grad_inner, grad_outer = refine(
        feature, cotangent, inner_weight, inner_bias, outer_weight, outer_bias, tile_margin
    )
    back_strip = lax.all_to_all(back_feature, "col", split_axis=0, concat_axis=1, tiled=True)
    flat_back = back_strip.reshape(TOK_DEV, JOIN_DIM)
    grad_project = lax.dot_general(
        tokens, flat_back, (((0,), (0,)), ((), ())), preferred_element_type=jnp.float32
    )
    grad_tokens = jnp.dot(flat_back, project_weight.T, preferred_element_type=jnp.float32).astype(
        jnp.bfloat16
    )
    row_sums = (
        lax.psum_scatter(
            grad_project.astype(jnp.bfloat16), "row", scatter_dimension=0, tiled=True
        ).astype(jnp.float32),
        lax.psum_scatter(
            grad_inner.astype(jnp.bfloat16), "row", scatter_dimension=2, tiled=True
        ).astype(jnp.float32),
        lax.psum_scatter(
            grad_outer.astype(jnp.bfloat16), "row", scatter_dimension=2, tiled=True
        ).astype(jnp.float32),
    )
    totals = (
        lax.psum_scatter(
            row_sums[0].astype(jnp.bfloat16), "col", scatter_dimension=1, tiled=True
        ).astype(jnp.float32),
        lax.psum_scatter(
            row_sums[1].astype(jnp.bfloat16), "col", scatter_dimension=3, tiled=True
        ).astype(jnp.float32),
        lax.psum_scatter(
            row_sums[2].astype(jnp.bfloat16), "col", scatter_dimension=3, tiled=True
        ).astype(jnp.float32),
    )
    return (refined, grad_tokens, totals[0] * scale, totals[1] * scale, totals[2] * scale)


def solution(mesh):
    in_specs = (
        P(("frame", "row", "col"), None),
        P(),
        P(),
        P(),
        P(),
        P(),
        P(),
        P(("frame", "row"), "col", None),
    )
    out_specs = (
        P(("frame", "row"), "col", None),
        P(("frame", "row", "col"), None),
        P(("frame", "row"), "col"),
        P("frame", None, "row", "col"),
        P("frame", None, "row", "col"),
    )
    return jax.shard_map(shards, mesh=mesh, in_specs=in_specs, out_specs=out_specs, check_vma=False)
```

profile of v0, /device:TPU:1, one launch (start us, length us, event | category | flops | bytes accessed | tf_op | source)
XLA Modules:
  0.0 493.2 jit_solution(16051983236068647464)
XLA Ops:
  8.0 1.3 collective-permute-start.9
  9.3 4.7 collective-permute-start.8
  14.1 2.3 fusion.3
  16.3 1.2 copy.213
  17.5 10.0 %all-to-all-start = ((bf16[2,256,384]{2,0,1:T(2,128)(2,1)}), bf16[2,256,384]{2,0,1:T(2,128)(2,1)S(1)}, u32[]{:S(2)}, u32[]{:S(2)}) async-start(bf16[2,256,384]{2,0,1:T(2,128)(2,1)} %copy.213), calls=%async_computation | async-start | bytes 786432 | tf_op jit(solution)/shard_map/all_to_all | solution.py:129
  27.8 2.1 collective-permute-start.10
  29.9 3.5 collective-permute-start.11
  33.5 2.3 fusion.72
  36.2 3.1 collective-permute-done.10
  39.3 1.6 pad_maximum_fusion.7
  42.1 1.3 fusion.69
  43.8 1.3 convolution_add_fusion.9
  46.7 4.0 collective-permute-start
  50.7 1.3 collective-permute-start.1
  52.3 3.0 collective-permute-done.1
  55.3 1.9 collective-permute-start.3
  57.2 4.2 collective-permute-start.2
  69.0 1.0 copy-done.4
  71.6 3.2 collective-permute-start.12
  74.8 1.3 collective-permute-start.13
  76.2 4.0 collective-permute-start.4
  80.2 1.3 collective-permute-start.5
  81.5 4.3 collective-permute-start.15
  85.9 1.9 collective-permute-start.14
  87.8 1.9 collective-permute-start.7
  89.8 3.8 collective-permute-start.6
  106.1 1.4 fusion.59
  107.6 24.2 %all_to_all.24 = bf16[32,16,384]{2,1,0:T(8,128)(2,1)S(1)} all-to-all(bf16[32,16,384]{2,1,0:T(8,128)(2,1)S(1)} %copy.246), channel_id=1, replica_groups=mesh['row'=8,'col'=16,'frame'=2] {'col'}, dimensions={0} | all-to-all | bytes 786432 | tf_op jit(solution)/shard_map/all_to_all | solution.py:139
  131.9 1.8 fusion
  133.7 2.4 copy.261
  141.9 2.3 copy.317
  144.2 4.4 reshape.230
  148.6 1.0 copy-done.10
  155.4 2.3 copy.316
  157.7 4.4 reshape.234
  162.2 12.5 %reduce-scatter.19.cloned.1.call-done = bf16[192,384]{1,0:T(8,128)(2,1)} async-done(((bf16[1536,384]{1,0:T(8,128)(2,1)}), bf16[192,384]{1,0:T(8,128)(2,1)}) %reduce-scatter.19.cloned.1.call-update) | async-done | bytes 147472
  174.7 1.7 copy.262
  176.7 70.1 %reduce-scatter.21.cloned.1.call-done = bf16[48,3456]{1,0:T(8,128)(2,1)} async-done(((bf16[384,3456]{1,0:T(8,128)(2,1)}), bf16[48,3456]{1,0:T(8,128)(2,1)}) %reduce-scatter.21.cloned.1.call-update) | async-done | bytes 331792
  246.8 1.1 reshape.231
  248.8 1.4 reshape.232
  251.1 63.6 %reduce-scatter.25.cloned.1.call-done = bf16[48,3456]{1,0:T(8,128)(2,1)} async-done(((bf16[384,3456]{1,0:T(8,128)(2,1)}), bf16[48,3456]{1,0:T(8,128)(2,1)}) %reduce-scatter.25.cloned.1.call-update) | async-done | bytes 331792
  314.7 1.1 reshape.235
  316.8 1.4 reshape.236
  318.2 3.4 convolution_convert_fusion
  321.6 48.5 %reduce-scatter.17.cloned.1.call-done = bf16[192,24]{0,1:T(8,128)(2,1)} async-done(((bf16[192,384]{0,1:T(8,128)(2,1)}), bf16[192,24]{0,1:T(8,128)(2,1)}) %reduce-scatter.17.cloned.1.call-update) | async-done | bytes 9232 | tf_op jit(solution)/shard_map/reduce_scatter | solution.py:159
  370.1 1.3 convert_multiply_fusion.2
  371.4 56.0 %reduce-scatter.23.cloned.1.call-done = bf16[24,432]{1,0:T(8,128)(2,1)} async-done(((bf16[384,432]{1,0:T(8,128)(2,1)}), bf16[24,432]{1,0:T(8,128)(2,1)}) %reduce-scatter.23.cloned.1.call-update) | async-done | bytes 20752
  429.0 55.7 %reduce-scatter.27.cloned.1.call-done = bf16[24,432]{1,0:T(8,128)(2,1)} async-done(((bf16[384,432]{1,0:T(8,128)(2,1)}), bf16[24,432]{1,0:T(8,128)(2,1)}) %reduce-scatter.27.cloned.1.call-update) | async-done | bytes 20752
  (213 shorter events, 44.0 us)
Async XLA Ops:
  7.2 6.9 %copy-start = (bf16[512,1536]{1,0:T(8,128)(2,1)S(1)}, bf16[512,1536]{1,0:T(8,128)(2,1)}, u32[]{:S(2)}) copy-start(bf16[512,1536]{1,0:T(8,128)(2,1)} %param.8) | copy-start | bytes 4718596
  8.0 19.5 %collective-permute-start.9 = (bf16[1,16,384]{2,1,0:T(8,128)(2,1)S(1)}, bf16[1,16,384]{2,1,0:T(8,128)(2,1)S(1)}, u32[]{:S(2)}, u32[]{:S(2)}) collective-permute-start(bf16[1,16,384]{2,1,0:T(8,128)(2,1)S(1)} %get-tuple-element.87), channel_id=1, source_target_pairs={{32,0},{64,32},{96,64},{128,96},{160,128},{192,160},{224,192},{33,... | collective-permute-start | bytes 36872 | tf_op jit(solution)/shard_map/ppermute | solution.py:23
  9.3 18.2 %copy-start.13 = (bf16[32,16,384]{2,1,0:T(8,128)(2,1)S(1)}, bf16[32,16,384]{2,1,0:T(8,128)(2,1)}, u32[]{:S(2)}) copy-start(bf16[32,16,384]{2,1,0:T(8,128)(2,1)} %param.15) | copy-start | bytes 1179652
  9.3 18.2 %collective-permute-start.8 = (bf16[1,16,384]{2,1,0:T(8,128)(2,1)S(1)}, bf16[1,16,384]{2,1,0:T(8,128)(2,1)S(1)}, u32[]{:S(2)}, u32[]{:S(2)}) collective-permute-start(bf16[1,16,384]{2,1,0:T(8,128)(2,1)S(1)} %get-tuple-element.88), channel_id=1, source_target_pairs={{0,32},{32,64},{64,96},{96,128},{128,160},{160,192},{192,224},{1,3... | collective-permute-start | bytes 36872 | tf_op jit(solution)/shard_map/ppermute | solution.py:20
  17.5 27.7 %all-to-all-start = ((bf16[2,256,384]{2,0,1:T(2,128)(2,1)}), bf16[2,256,384]{2,0,1:T(2,128)(2,1)S(1)}, u32[]{:S(2)}, u32[]{:S(2)}) async-start(bf16[2,256,384]{2,0,1:T(2,128)(2,1)} %copy.213), calls=%async_computation | async-start | bytes 786432 | tf_op jit(solution)/shard_map/all_to_all | solution.py:129
  27.4 147.3 %reduce-scatter.19.cloned.1.call-start = ((), (), s32[]{:S(2)}) async-start(), calls=%async_computation.9 | async-start | bytes 1327104
  27.5 8.3 %copy-start.3 = (bf16[3,3,384,384]{3,2,1,0:T(8,128)(2,1)S(1)}, bf16[3,3,384,384]{3,2,1,0:T(8,128)(2,1)}, u32[]{:S(2)}) copy-start(bf16[3,3,384,384]{3,2,1,0:T(8,128)(2,1)} %param.13) | copy-start | bytes 7962628
  27.8 11.5 %collective-permute-start.10 = (bf16[34,1,384]{2,1,0:T(2,128)(2,1)S(1)}, bf16[34,1,384]{2,1,0:T(2,128)(2,1)S(1)}, u32[]{:S(2)}, u32[]{:S(2)}) collective-permute-start(bf16[34,1,384]{2,1,0:T(2,128)(2,1)S(1)} %get-tuple-element.78), channel_id=1, source_target_pairs={{2,0},{4,2},{6,4},{8,6},{10,8},{12,10},{14,12},{16,14},{18,16},{20... | collective-permute-start | bytes 78344 | tf_op jit(solution)/shard_map/ppermute | solution.py:23
  29.9 9.4 %collective-permute-start.11 = (bf16[34,1,384]{2,1,0:T(2,128)(2,1)S(1)}, bf16[34,1,384]{2,1,0:T(2,128)(2,1)S(1)}, u32[]{:S(2)}, u32[]{:S(2)}) collective-permute-start(bf16[34,1,384]{2,1,0:T(2,128)(2,1)S(1)} %get-tuple-element.79), channel_id=1, source_target_pairs={{0,2},{2,4},{4,6},{6,8},{8,10},{10,12},{12,14},{14,16},{16,18},{18... | collective-permute-start | bytes 78344 | tf_op jit(solution)/shard_map/ppermute | solution.py:20
  46.7 5.6 %collective-permute-start = (bf16[1,16,384]{2,0,1:T(2,128)(2,1)S(1)}, bf16[1,16,384]{2,0,1:T(2,128)(2,1)S(1)}, u32[]{:S(2)}, u32[]{:S(2)}) collective-permute-start(bf16[1,16,384]{2,0,1:T(2,128)(2,1)S(1)} %get-tuple-element.95), channel_id=1, source_target_pairs={{0,32},{32,64},{64,96},{96,128},{128,160},{160,192},{192,224},{1,3... | collective-permute-start | bytes 36872 | tf_op jit(solution)/shard_map/ppermute | solution.py:20
  50.7 4.6 collective-permute-start.1
  52.3 14.5 %copy-start.27 = (bf16[16,2,16,384]{3,2,1,0:T(8,128)(2,1)}, bf16[16,2,16,384]{3,2,1,0:T(8,128)(2,1)S(1)}, u32[]{:S(2)}) copy-start(bf16[16,2,16,384]{3,2,1,0:T(8,128)(2,1)S(1)} %copy.220) | copy-start | bytes 1179652
  55.3 6.7 %collective-permute-start.3 = (bf16[34,1,384]{2,0,1:T(8,128)(2,1)S(1)}, bf16[34,1,384]{2,0,1:T(8,128)(2,1)S(1)}, u32[]{:S(2)}, u32[]{:S(2)}) collective-permute-start(bf16[34,1,384]{2,0,1:T(8,128)(2,1)S(1)} %get-tuple-element.73), channel_id=1, source_target_pairs={{2,0},{4,2},{6,4},{8,6},{10,8},{12,10},{14,12},{16,14},{18,16},{20... | collective-permute-start | bytes 78344 | tf_op jit(solution)/shard_map/ppermute | solution.py:23
  57.2 5.4 %collective-permute-start.2 = (bf16[34,1,384]{2,0,1:T(8,128)(2,1)S(1)}, bf16[34,1,384]{2,0,1:T(8,128)(2,1)S(1)}, u32[]{:S(2)}, u32[]{:S(2)}) collective-permute-start(bf16[34,1,384]{2,0,1:T(8,128)(2,1)S(1)} %get-tuple-element.74), channel_id=1, source_target_pairs={{0,2},{2,4},{4,6},{6,8},{8,10},{10,12},{12,14},{14,16},{16,18},{18... | collective-permute-start | bytes 78344 | tf_op jit(solution)/shard_map/ppermute | solution.py:20
  63.5 1.8 copy-start.2
  67.6 1.3 copy-start.31
  67.7 1.3 copy-start.32
  68.1 1.8 copy-start.4
  68.1 2.0 copy-start.29
  68.1 2.2 copy-start.30
  68.1 2.2 copy-start.36
  70.9 31.3 %copy-start.33 = (bf16[512,384]{1,0:T(8,128)(2,1)}, bf16[512,384]{1,0:T(8,128)(2,1)S(1)}, u32[]{:S(2)}) copy-start(bf16[512,384]{1,0:T(8,128)(2,1)S(1)} %get-tuple-element.97) | copy-start | bytes 1179652
  71.5 25.6 %copy-start.5 = (bf16[32,16,384]{2,0,1:T(8,128)(2,1)}, bf16[32,16,384]{2,0,1:T(8,128)(2,1)S(1)}, u32[]{:S(2)}) copy-start(bf16[32,16,384]{2,0,1:T(8,128)(2,1)S(1)} %get-tuple-element.36) | copy-start | bytes 1179652
  71.6 9.8 %collective-permute-start.12 = (bf16[1,16,384]{2,0,1:T(2,128)(2,1)S(1)}, bf16[1,16,384]{2,0,1:T(2,128)(2,1)S(1)}, u32[]{:S(2)}, u32[]{:S(2)}) collective-permute-start(bf16[1,16,384]{2,0,1:T(2,128)(2,1)S(1)} %get-tuple-element.82), channel_id=1, source_target_pairs={{0,32},{32,64},{64,96},{96,128},{128,160},{160,192},{192,224},{1,3... | collective-permute-start | bytes 36872 | tf_op jit(solution)/shard_map/ppermute | solution.py:20
  74.8 6.7 %collective-permute-start.13 = (bf16[1,16,384]{2,0,1:T(2,128)(2,1)S(1)}, bf16[1,16,384]{2,0,1:T(2,128)(2,1)S(1)}, u32[]{:S(2)}, u32[]{:S(2)}) collective-permute-start(bf16[1,16,384]{2,0,1:T(2,128)(2,1)S(1)} %get-tuple-element.83), channel_id=1, source_target_pairs={{32,0},{64,32},{96,64},{128,96},{160,128},{192,160},{224,192},{33,... | collective-permute-start | bytes 36872 | tf_op jit(solution)/shard_map/ppermute | solution.py:23
  76.2 11.6 %collective-permute-start.4 = (bf16[1,16,384]{2,0,1:T(2,128)(2,1)S(1)}, bf16[1,16,384]{2,0,1:T(2,128)(2,1)S(1)}, u32[]{:S(2)}, u32[]{:S(2)}) collective-permute-start(bf16[1,16,384]{2,0,1:T(2,128)(2,1)S(1)} %get-tuple-element.91), channel_id=1, source_target_pairs={{0,32},{32,64},{64,96},{96,128},{128,160},{160,192},{192,224},{1,3... | collective-permute-start | bytes 36872 | tf_op jit(solution)/shard_map/ppermute | solution.py:20
  80.2 7.6 %collective-permute-start.5 = (bf16[1,16,384]{2,0,1:T(2,128)(2,1)S(1)}, bf16[1,16,384]{2,0,1:T(2,128)(2,1)S(1)}, u32[]{:S(2)}, u32[]{:S(2)}) collective-permute-start(bf16[1,16,384]{2,0,1:T(2,128)(2,1)S(1)} %get-tuple-element.92), channel_id=1, source_target_pairs={{32,0},{64,32},{96,64},{128,96},{160,128},{192,160},{224,192},{33,... | collective-permute-start | bytes 36872 | tf_op jit(solution)/shard_map/ppermute | solution.py:23
  81.5 13.2 %collective-permute-start.15 = (bf16[34,1,384]{2,0,1:T(8,128)(2,1)S(1)}, bf16[34,1,384]{2,0,1:T(8,128)(2,1)S(1)}, u32[]{:S(2)}, u32[]{:S(2)}) collective-permute-start(bf16[34,1,384]{2,0,1:T(8,128)(2,1)S(1)} %get-tuple-element.65), channel_id=1, source_target_pairs={{0,2},{2,4},{4,6},{6,8},{8,10},{10,12},{12,14},{14,16},{16,18},{18... | collective-permute-start | bytes 78344 | tf_op jit(solution)/shard_map/ppermute | solution.py:20
  85.9 9.2 %collective-permute-start.14 = (bf16[34,1,384]{2,0,1:T(8,128)(2,1)S(1)}, bf16[34,1,384]{2,0,1:T(8,128)(2,1)S(1)}, u32[]{:S(2)}, u32[]{:S(2)}) collective-permute-start(bf16[34,1,384]{2,0,1:T(8,128)(2,1)S(1)} %get-tuple-element.66), channel_id=1, source_target_pairs={{2,0},{4,2},{6,4},{8,6},{10,8},{12,10},{14,12},{16,14},{18,16},{20... | collective-permute-start | bytes 78344 | tf_op jit(solution)/shard_map/ppermute | solution.py:23
  87.8 9.3 %collective-permute-start.7 = (bf16[34,1,384]{2,0,1:T(8,128)(2,1)S(1)}, bf16[34,1,384]{2,0,1:T(8,128)(2,1)S(1)}, u32[]{:S(2)}, u32[]{:S(2)}) collective-permute-start(bf16[34,1,384]{2,0,1:T(8,128)(2,1)S(1)} %get-tuple-element.69), channel_id=1, source_target_pairs={{2,0},{4,2},{6,4},{8,6},{10,8},{12,10},{14,12},{16,14},{18,16},{20... | collective-permute-start | bytes 78344 | tf_op jit(solution)/shard_map/ppermute | solution.py:23
  89.8 7.4 %collective-permute-start.6 = (bf16[34,1,384]{2,0,1:T(8,128)(2,1)S(1)}, bf16[34,1,384]{2,0,1:T(8,128)(2,1)S(1)}, u32[]{:S(2)}, u32[]{:S(2)}) collective-permute-start(bf16[34,1,384]{2,0,1:T(8,128)(2,1)S(1)} %get-tuple-element.70), channel_id=1, source_target_pairs={{0,2},{2,4},{4,6},{6,8},{8,10},{10,12},{12,14},{14,16},{16,18},{18... | collective-permute-start | bytes 78344 | tf_op jit(solution)/shard_map/ppermute | solution.py:20
  131.9 4.3 copy-start.16
  133.7 2.5 copy-start.12
  136.2 110.6 %reduce-scatter.21.cloned.1.call-start = ((), (), s32[]{:S(2)}) async-start(), calls=%async_computation.10 | async-start | bytes 2985984
  138.0 1.1 copy-start.34
  148.6 1.0 copy-start.10
  148.6 1.2 copy-start.15
  148.6 1.5 copy-start.26
  148.6 166.2 %reduce-scatter.25.cloned.1.call-start = ((), (), s32[]{:S(2)}) async-start(), calls=%async_computation.12 | async-start | bytes 2985984
  150.1 1.0 copy-start.8
  151.6 1.0 copy-start.6
  153.5 1.0 copy-start.24
  162.1 88.2 %copy-start.18 = (bf16[32,16,384]{2,0,1:T(8,128)(2,1)S(1)}, bf16[32,16,384]{2,0,1:T(8,128)(2,1)}, u32[]{:S(2)}) copy-start(bf16[32,16,384]{2,0,1:T(8,128)(2,1)} %get-tuple-element.38) | copy-start | bytes 1179652
  162.1 208.0 %reduce-scatter.17.cloned.1.call-start = ((), (), s32[]{:S(2)}) async-start(), calls=%async_computation.8 | async-start | bytes 208896 | tf_op jit(solution)/shard_map/reduce_scatter | solution.py:159
  176.4 251.0 %reduce-scatter.23.cloned.1.call-start = ((), (), s32[]{:S(2)}) async-start(), calls=%async_computation.11 | async-start | bytes 417792
  250.2 68.0 %copy-start.17 = (bf16[2,16,16,384]{3,2,1,0:T(8,128)(2,1)S(1)}, bf16[2,16,16,384]{3,2,1,0:T(8,128)(2,1)}, u32[]{:S(2)}) copy-start(bf16[2,16,16,384]{3,2,1,0:T(8,128)(2,1)} %copy-done.16) | copy-start | bytes 1179652
  250.2 234.4 %reduce-scatter.27.cloned.1.call-start = ((), (), s32[]{:S(2)}) async-start(), calls=%async_computation.13 | async-start | bytes 417792
  316.8 169.3 %copy-start.1 = (bf16[512,1536]{1,0:T(8,128)(2,1)S(1)}, bf16[512,1536]{1,0:T(8,128)(2,1)}, u32[]{:S(2)}) copy-start(bf16[512,1536]{1,0:T(8,128)(2,1)} %param.8) | copy-start | bytes 4718596
  (12 other events, 11.0 us)
Sparse Core Ops, SparseCore 0:
  136.3 38.3 reduce-scatter.18
  177.2 69.4 reduce-scatter.20
  249.4 65.3 reduce-scatter.24
  317.1 52.9 reduce-scatter.16
  372.6 54.7 reduce-scatter.22
  429.8 54.7 reduce-scatter.26
where the time goes:
time: 502 us; the launch traced here: 493 us
  waiting for transfers between devices  313 us (62%)
  starting transfers between devices  55.3 us (11%)
  local copies, waits for them, and re-layouts  43 us (9%)
  matrix products  33.7 us (7%)
  blocking collectives  24.2 us (5%)
  between operations  15.8 us (3%)
  other arithmetic  8.74 us (2%)
    unnamed x11, waiting for transfers between devices  258 us
    reduce_scatter x1, waiting for transfers between devices, shards(): lax.psum_scatter(row_sums[0].astype(jnp.bfloat16), 'col', scatter_dimensi...  48.5 us
    unnamed x90, local copies, waits for them, and re-layouts  34.8 us
    ppermute x8, starting transfers between devices, with_halo(): lax.ppermute(lax.slice_in_dim(block, block.shape[dim] - width, None, axis...  31.8 us
    all_to_all x1, blocking collectives, shards(): lax.all_to_all(back_feature, 'col', split_axis=0, concat_axis=1, tiled=True)  24.2 us
    ppermute x8, starting transfers between devices, with_halo(): lax.ppermute(lax.slice_in_dim(block, 0, width, axis=dim), axis, backward)  13.1 us
    dot_general x18, matrix products, conv_transpose(): jnp.dot(window, kernel[top, left].T, preferred_element_type=jnp.float32)  11.2 us
  transfers between devices with their start and end apart: 23, of which 8 were waited for; matrix products, arithmetic and copies ran while one was open for 11% of the time, Pallas kernels for 0%

commit v1 on v0

v1 whole, which is shorter than its diff:
```python
import math

import jax
import jax.numpy as jnp
from jax import lax
from jax.experimental import pallas as pl
from jax.experimental.pallas import tpu as pltpu
from jax.sharding import PartitionSpec as P

VIT = 1536
DIM = 384
WIDE = 3 * DIM
COLS = 256
TOK = 512
TILE_ROWS = 32
TILE_COLS = 16
NY = 4
NX = 2
NZ = 8
NCOL = 16
NROW = 8
BF = jnp.bfloat16
F32 = jnp.float32
MESH = pl.DeviceIdType.MESH

ROW_PIECES = (
    ("o1", 96, 48, (3, 4, 5)),
    ("o2", 144, 144, (0, 1, 2, 6, 7, 8)),
    ("i1", 48, 96, (3, 4, 5)),
    ("i2", 144, 144, (0, 1, 2, 6, 7, 8)),
    ("p", 96, 96, ()),
)
Z_PIECES = (("zo", 256), ("zi", 256), ("zp", 128))
CORE, XAX, YAX, NROWSEM = 0, 1, 2, 8
SWAP, NZSEM = 7, 8


def scratch_table():
    table = {
        "tok": ((TOK, VIT), BF),
        "tok_t": ((VIT, TOK), BF),
        "wp": ((VIT, DIM), BF),
        "wi": ((3, WIDE, DIM), BF),
        "wo": ((3, WIDE, DIM), BF),
        "act": ((4, COLS, DIM), BF),
        "hid": ((4, COLS, DIM), BF),
        "cot": ((4, COLS, DIM), BF),
        "bh": ((4, COLS, DIM), BF),
        "ea": ((4 * COLS, WIDE), BF),
        "eh": ((4 * COLS, WIDE), BF),
        "ec": ((4 * COLS, WIDE), BF),
        "feat": ((TOK, DIM), BF),
        "bf": ((TOK, DIM), BF),
        "slope": ((TOK, DIM), F32),
        "act_t": ((DIM, TOK), BF),
        "hid_t": ((DIM, TOK), BF),
        "strip": ((2, COLS, DIM), BF),
        "tile": ((TILE_ROWS, TILE_COLS, DIM), BF),
        "gtok": ((TOK, VIT), BF),
    }
    for name, n0, n1, _ in ROW_PIECES:
        nm = max(n0, n1)
        table |= {
            name + "_part": ((NROW, n0 + n1, DIM), BF),
            name + "_core": ((NROW, nm, DIM), BF),
            name + "_sum": ((NY, NX, nm, DIM), BF),
            name + "_xr": ((NY, nm, DIM), BF),
            name + "_sx": ((NY, nm, DIM), BF),
            name + "_yr": ((6, nm, DIM), BF),
            name + "_fw": ((2, nm, DIM), BF),
        }
    for name, lanes in Z_PIECES:
        table |= {
            name + "_red": ((lanes, DIM), F32),
            name + "_zs": ((NZ, DIM // NZ, lanes), BF),
            name + "_zr": ((NZ - 1, DIM // NZ, lanes), BF),
            name + "_fs": ((2, DIM // NCOL, lanes), F32),
            name + "_fr": ((DIM // NCOL, lanes), F32),
        }
    out = {k: pltpu.VMEM(*v) for k, v in table.items()}
    for group, count in ((ROW_PIECES, NROWSEM), (Z_PIECES, NZSEM)):
        for piece in group:
            out[piece[0] + "_ss"] = pltpu.SemaphoreType.DMA((count,))
            out[piece[0] + "_rs"] = pltpu.SemaphoreType.DMA((count,))
    out["load"] = pltpu.SemaphoreType.DMA((10,))
    out["halo_ss"] = pltpu.SemaphoreType.DMA((8,))
    out["halo_rs"] = pltpu.SemaphoreType.DMA((8,))
    out["swap_ss"] = pltpu.SemaphoreType.DMA((30,))
    out["swap_rs"] = pltpu.SemaphoreType.DMA((30,))
    return out


def dot(a, b):
    return jnp.dot(a, b, preferred_element_type=F32)


def dot_nt(a, b):
    return lax.dot_general(a, b, (((1,), (1,)), ((), ())), preferred_element_type=F32)


def silu(v):
    return v * jax.nn.sigmoid(v)


def silu_slope(v):
    s = jax.nn.sigmoid(v)
    return s * (1.0 + v * (1.0 - s))


class Where:
    def __init__(self):
        self.r = lax.axis_index("row")
        self.c = lax.axis_index("col")
        self.y = self.r // 2
        self.x = self.r % 2
        self.z = self.c // 2
        self.core = self.c % 2
        here = self.r * NCOL + self.c
        above = (here + NROW * NCOL - 1) % (NROW * NCOL)
        below = (here + 1) % (NROW * NCOL)
        self.up = {"row": above // NCOL, "col": above % NCOL}
        self.down = {"row": below // NCOL, "col": below % NCOL}
        self.first = here == 0
        self.last = here == NROW * NCOL - 1
        self.pair = {"col": self.z * 2 + 1 - self.core}
        self.across = {"row": self.y * 2 + 1 - self.x}

    def at_y(self, k):
        return {"row": ((self.y + k) % NY) * 2 + self.x}

    def at_z(self, k):
        return {"col": ((self.z + k) % NZ) * 2 + self.core}

    def at_col(self, k):
        return {"col": (self.c + k) % NCOL}


def remote(src, dst, ss, rs, device):
    return pltpu.make_async_remote_copy(
        src_ref=src, dst_ref=dst, send_sem=ss, recv_sem=rs, device_id=device, device_id_type=MESH
    )


def per_core(w, step):
    for k in (0, 1):
        pl.when(w.core == k)(lambda k=k: step(k))


class RowPiece:
    def __init__(self, w, m, name, n0, n1, red, at):
        self.w = w
        self.n = (n0, n1)
        self.off = (0, n0)
        self.out = (red, at)
        for field in ("part", "core", "sum", "xr", "sx", "yr", "fw", "ss", "rs"):
            setattr(self, field, m[name + "_" + field])

    def copy(self, src, dst, k, device):
        return remote(src, dst, self.ss.at[k], self.rs.at[k], device)

    def core_out(self, k):
        o, m = self.off[1 - k], self.n[1 - k]
        return self.copy(self.part.at[:, o : o + m], self.core.at[:, :m], CORE, self.w.pair)

    def core_in(self, k):
        n = self.n[k]
        return self.copy(self.core.at[:, :n], self.core.at[:, :n], CORE, self.w.pair)

    def stage0(self):
        per_core(self.w, lambda k: self.core_out(k).start())

    def x_copy(self, k):
        n = self.n[k]
        if k == 0:
            src, dst = self.sum.at[:, 1 - self.w.x, :n], self.xr.at[:, :n]
        else:
            src, dst = self.sx.at[1 - self.w.x, :n], self.xr.at[0, :n]
        return self.copy(src, dst, XAX, self.w.across)

    def halves(self, k):
        n = self.n[k]
        if k == 1:
            return (pl.ds(0, n), pl.ds(0, n))
        low = (n // 32) * 16
        return (pl.ds(0, low), pl.ds(low, n - low))

    def block(self, k, t, h):
        if k == 1:
            return self.sum.at[t, h, pl.ds(0, self.n[1])]
        return self.sx.at[t, self.halves(0)[h]]

    def slot(self, k, s, h):
        return self.yr.at[s, pl.ds(0, self.halves(k)[h].size)]

    def forward(self, k, h):
        return self.fw.at[h, pl.ds(0, self.halves(k)[h].size)]

    def y_copy(self, k, j):
        w = self.w
        far, before, after = (w.y + 2) % NY, (w.y + 3) % NY, (w.y + 1) % NY
        h = j % 2
        step = (1, 3, 3, 1, 1, 3)[j]
        if j < 4:
            src = self.block(k, (far, far, before, after)[j], h)
        else:
            src = self.forward(k, h)
        return self.copy(src, self.slot(k, j, h), YAX + j, w.at_y(step))

    def y_first(self, k):
        for j in range(4):
            self.y_copy(k, j).start()

    def y_second(self, k):
        for h, t in ((0, (self.w.y + 1) % NY), (1, (self.w.y + 3) % NY)):
            self.y_copy(k, h).wait_recv()
            self.forward(k, h)[...] = self.block(k, t, h)[...] + self.slot(k, h, h)[...]
            self.y_copy(k, 4 + h).start()

    def y_end(self, k, h):
        self.y_copy(k, 2 + h).wait_recv()
        self.y_copy(k, 4 + h).wait_recv()
        return (
            self.block(k, self.w.y, h)[...].astype(F32)
            + self.slot(k, 4 + h, h)[...].astype(F32)
            + self.slot(k, 2 + h, h)[...].astype(F32)
        )

    def stage1(self):
        def step(k):
            n, o = self.n[k], self.off[k]
            self.core_in(k).wait_recv()
            for j in range(NROW):
                self.sum[j // NX, j % NX, :n] = self.part[j, o : o + n] + self.core[j, :n]
            if k == 0:
                self.x_copy(0).start()
            else:
                self.y_first(1)

        per_core(self.w, step)

    def stage2(self):
        def step(k):
            if k == 0:
                n = self.n[0]
                self.x_copy(0).wait_recv()
                for t in range(NY):
                    self.sx[t, :n] = self.sum[t, self.w.x, :n] + self.xr[t, :n]
                self.y_first(0)
            else:
                self.y_second(1)

        per_core(self.w, step)

    def stage3(self):
        def step(k):
            if k == 0:
                self.y_second(0)
            else:
                for h in (0, 1):
                    self.sx[h, : self.n[1]] = self.y_end(1, h).astype(BF)
                self.x_copy(1).start()

        per_core(self.w, step)

    def stage4(self):
        def step(k):
            red, at = self.out[0], self.out[1][k]
            n = self.n[k]
            if k == 0:
                for h in (0, 1):
                    rows = self.halves(0)[h]
                    red[at + rows.start : at + rows.start + rows.size] = self.y_end(0, h)
            else:
                self.x_copy(1).wait_recv()
                red[at : at + n] = self.sx[self.w.x, :n].astype(F32) + self.xr[0, :n].astype(F32)

        per_core(self.w, step)

    def finish(self):
        def step(k):
            self.core_out(k).wait_send()
            self.x_copy(k).wait_send()
            for j in range(6):
                self.y_copy(k, j).wait_send()

        per_core(self.w, step)


class ZPiece:
    def __init__(self, w, m, name, lanes, rows):
        self.w = w
        self.lanes = lanes
        self.rows = rows
        for field in ("red", "zs", "zr", "fs", "fr", "ss", "rs"):
            setattr(self, field, m[name + "_" + field])

    def copy(self, d):
        w = self.w
        if d == 0:
            src, dst, k, device = self.fs.at[1 - w.core], self.fr, SWAP, w.pair
        else:
            src, dst, k, device = self.zs.at[(w.z + d) % NZ], self.zr.at[d - 1], d - 1, w.at_z(d)
        return remote(src, dst, self.ss.at[k], self.rs.at[k], device)

    def clear(self):
        low = min(self.rows)
        self.red[low:] = jnp.zeros((self.lanes - low, DIM), F32)

    def stage4(self):
        self.zs[...] = self.red[...].T.astype(BF).reshape(NZ, DIM // NZ, self.lanes)
        for d in (4, 3, 5, 2, 6, 1, 7):
            self.copy(d).start()

    def stage5(self):
        total = self.zs[self.w.z].astype(F32)
        for d in range(1, NZ):
            self.copy(d).wait_recv()
            total = total + self.zr[d - 1].astype(F32)
        self.fs[...] = total.reshape(2, DIM // NCOL, self.lanes)
        self.copy(0).start()

    def stage6(self, put):
        self.copy(0).wait_recv()

        def step(k):
            put(k, self.fs[k])
            put(1 - k, self.fr[...])

        per_core(self.w, step)

    def finish(self):
        for d in range(NZ):
            self.copy(d).wait_send()


def kernel(names, scale, *refs):
    tok_h, wp_h, bp, wi_h, bi, wo_h, bo, cot_h = refs[:8]
    refined_o, gtok_o, gproj_o, gin_o, gout_o = refs[8:13]
    m = dict(zip(names, refs[13:]))
    w = Where()
    share, width = DIM // NCOL, DIM // NROW
    zo = ZPiece(w, m, "zo", 256, (240, 192))
    zi = ZPiece(w, m, "zi", 256, (192, 240))
    zp = ZPiece(w, m, "zp", 128, (96, 96))
    places = {"o1": (zo, (0, 0)), "o2": (zo, (96, 48)), "i1": (zi, (0, 0)), "i2": (zi, (48, 96)), "p": (zp, (0, 0))}
    rows, taps = {}, {}
    for name, n0, n1, taps[name] in ROW_PIECES:
        target, at = places[name]
        rows[name] = RowPiece(w, m, name, n0, n1, target.red, at)
    o1, o2, i1, i2, pp = rows.values()

    barrier = pltpu.get_barrier_semaphore()
    friends = [w.at_col(k) for k in range(1, NCOL)]
    friends += [w.across, w.at_y(1), w.at_y(3), w.up, w.down]
    for device in friends:
        pl.semaphore_signal(barrier, inc=1, device_id=device, device_id_type=MESH)

    load = m["load"]
    loads = [
        pltpu.make_async_copy(src, m[dst], load.at[k])
        for k, (src, dst) in enumerate(((tok_h, "tok"), (wp_h, "wp"), (wi_h, "wi"), (wo_h, "wo")))
    ]
    loads[0].start()
    loads[1].start()
    here = pl.ds(pl.multiple_of(w.c * TILE_COLS, TILE_COLS), TILE_COLS)
    mine = pl.ds(w.c * 2, 2)
    cot = m["cot"]

    def halo(center, k):
        up = remote(center.at[1], center.at[3], m["halo_ss"].at[k], m["halo_rs"].at[k], w.up)
        down = remote(center.at[2], center.at[0], m["halo_ss"].at[k + 1], m["halo_rs"].at[k + 1], w.down)
        up.start()
        down.start()
        return [down, up]

    keep_low = jnp.where(w.first, 0.0, 1.0).astype(F32)
    keep_high = jnp.where(w.last, 0.0, 1.0).astype(F32)

    def expand(center, wide, row, flip):
        v = center[row].astype(F32)
        if row == 0:
            v = v * keep_low
        if row == 3:
            v = v * keep_high
        at = lax.broadcasted_iota(jnp.int32, (COLS, DIM), 0)
        before = jnp.where(at == 0, 0.0, pltpu.roll(v, 1, 0))
        after = jnp.where(at == COLS - 1, 0.0, pltpu.roll(v, COLS - 1, 0))
        first, last = (after, before) if flip else (before, after)
        rows = pl.ds(row * COLS, COLS)
        wide[rows, 0:DIM] = first.astype(BF)
        wide[rows, DIM : 2 * DIM] = v.astype(BF)
        wide[rows, 2 * DIM : WIDE] = last.astype(BF)

    def expand_rim(center, wide, copies, flip):
        copies[0].wait_recv()
        expand(center, wide, 0, flip)
        copies[1].wait_recv()
        expand(center, wide, 3, flip)

    def conv(wide, kern):
        total = dot(wide[0:TOK], kern[0])
        total = total + dot(wide[COLS : COLS + TOK], kern[1])
        return total + dot(wide[2 * COLS : 2 * COLS + TOK], kern[2])

    def conv_t(wide, kern):
        total = jnp.zeros((TOK, DIM), F32)
        for a in range(3):
            at = slice((2 - a) * COLS, (2 - a) * COLS + TOK)
            for b in range(3):
                lanes = slice(b * DIM, (b + 1) * DIM)
                total = total + dot_nt(wide[at, lanes], kern[a, lanes])
        return total

    def weight_grad(left_t, wide, name):
        for a in sorted({t // 3 for t in taps[name]}):
            g = dot(left_t[...], wide[(2 - a) * COLS : (2 - a) * COLS + TOK])
            for b in range(3):
                at = taps[name].index(3 * a + b) * width
                rows[name].part[:, at : at + width] = (
                    g[:, b * DIM : (b + 1) * DIM].astype(BF).reshape(NROW, width, DIM)
                )

    act, hid, bh = m["act"], m["hid"], m["bh"]
    loads[0].wait()
    loads[1].wait()
    loads[2].start()
    own_cot = pltpu.make_async_copy(cot_h.at[mine], cot.at[pl.ds(1, 2), here], load.at[4])
    own_cot.start()
    feature = (dot(m["tok"][...], m["wp"][...]) + bp[...][None, :]).astype(BF)
    m["feat"][...] = feature
    activated = silu(feature.astype(F32)).astype(BF)
    act[1:3] = activated.reshape(2, COLS, DIM)

    pl.semaphore_wait(barrier, len(friends))

    act_halo = halo(act, 0)
    cot_copies = []
    for k in range(1, NCOL):
        there = (w.c + k) % NCOL
        cot_copies.append(
            remote(
                cot_h.at[pl.ds(there * 2, 2)],
                cot.at[pl.ds(1, 2), here],
                m["swap_ss"].at[k - 1],
                m["swap_rs"].at[k - 1],
                w.at_col(k),
            )
        )
        cot_copies[-1].start()
    loads[3].start()
    for z in (zo, zi, zp):
        z.clear()
    m["act_t"][...] = act[1:3].reshape(TOK, DIM).T
    expand(act, m["ea"], 1, False)
    expand(act, m["ea"], 2, False)
    m["tok_t"][...] = m["tok"][...].T
    expand_rim(act, m["ea"], act_halo, False)

    loads[2].wait()
    pre = conv(m["ea"], m["wi"]) + bi[...][None, :]
    hidden = silu(pre).astype(BF)
    m["slope"][...] = silu_slope(pre)
    hid[1:3] = hidden.reshape(2, COLS, DIM)
    hid_halo = halo(hid, 2)
    m["hid_t"][...] = hid[1:3].reshape(TOK, DIM).T
    expand(hid, m["eh"], 1, False)
    expand(hid, m["eh"], 2, False)

    own_cot.wait()
    for c in cot_copies:
        c.wait_recv()
    cot_halo = halo(cot, 4)
    expand(cot, m["ec"], 1, True)
    expand(cot, m["ec"], 2, True)
    weight_grad(m["hid_t"], m["ec"], "o1")
    o1.stage0()
    expand_rim(hid, m["eh"], hid_halo, False)
    loads[3].wait()
    refined = m["feat"][...].astype(F32) + conv(m["eh"], m["wo"]) + bo[...][None, :]
    m["strip"][...] = refined.astype(BF).reshape(2, COLS, DIM)
    o1.stage1()
    expand_rim(cot, m["ec"], cot_halo, True)

    bh[1:3] = (conv_t(m["ec"], m["wo"]) * m["slope"][...]).astype(BF).reshape(2, COLS, DIM)
    bh_halo = halo(bh, 6)
    weight_grad(m["hid_t"], m["ec"], "o2")
    o2.stage0()
    expand(bh, m["ea"], 1, True)
    expand(bh, m["ea"], 2, True)
    weight_grad(m["act_t"], m["ea"], "i1")
    i1.stage0()
    o1.stage2()
    o2.stage1()
    expand_rim(bh, m["ea"], bh_halo, True)

    own_refined = pltpu.make_async_copy(m["strip"].at[:, here], m["tile"].at[mine], load.at[5])
    own_refined.start()
    refined_copies = []
    for k in range(1, NCOL):
        there = (w.c + k) % NCOL
        refined_copies.append(
            remote(
                m["strip"].at[:, pl.ds(pl.multiple_of(there * TILE_COLS, TILE_COLS), TILE_COLS)],
                m["tile"].at[mine],
                m["swap_ss"].at[14 + k],
                m["swap_rs"].at[14 + k],
                w.at_col(k),
            )
        )
        refined_copies[-1].start()

    i1.stage1()
    weight_grad(m["act_t"], m["ea"], "i2")
    i2.stage0()
    o1.stage3()
    back = conv_t(m["ea"], m["wi"]) * silu_slope(m["feat"][...].astype(F32))
    back_feature = (cot[1:3].reshape(TOK, DIM).astype(F32) + back).astype(BF)
    m["bf"][...] = back_feature
    o2.stage2()
    i2.stage1()
    pp.part[...] = dot(m["tok_t"][...], m["bf"][...]).astype(BF).reshape(NROW, VIT // NROW, DIM)
    pp.stage0()
    i1.stage2()
    o1.stage4()
    o2.stage3()
    pp.stage1()
    i1.stage3()
    m["gtok"][...] = dot_nt(m["bf"][...], m["wp"][...]).astype(BF)
    gtok_copy = pltpu.make_async_copy(m["gtok"], gtok_o, load.at[6])
    gtok_copy.start()
    o2.stage4()
    zo.stage4()
    i2.stage2()
    i1.stage4()
    pp.stage2()
    i2.stage3()
    pp.stage3()
    i2.stage4()
    zi.stage4()
    pp.stage4()
    zp.stage4()
    zo.stage5()
    own_refined.wait()
    for c in refined_copies:
        c.wait_recv()
    refined_copy = pltpu.make_async_copy(m["tile"], refined_o, load.at[7])
    refined_copy.start()
    zi.stage5()
    zp.stage5()

    def put_taps(out, order):
        def put(k, value):
            for j, t in enumerate(order[k]):
                out[t] = value[:, j * width : (j + 1) * width] * scale

        return put

    def put_project(k, value):
        gproj_o[:, k * 96 : (k + 1) * 96] = value[:, :96] * scale

    zo.stage6(put_taps(gout_o, ((3, 4, 0, 1, 2), (5, 6, 7, 8))))
    zi.stage6(put_taps(gin_o, ((3, 0, 1, 2), (4, 5, 6, 7, 8))))
    zp.stage6(put_project)

    for c in act_halo + hid_halo + cot_halo + bh_halo + cot_copies + refined_copies:
        c.wait_send()
    for p in (o1, o2, i1, i2, pp, zo, zi, zp):
        p.finish()
    gtok_copy.wait()
    refined_copy.wait()


def hand_over(*refs):
    src, dst, via, sem = refs[:5], refs[5:10], refs[10:15], refs[15]
    into = [pltpu.make_async_copy(src[k], via[k], sem.at[k]) for k in range(5)]
    out = [pltpu.make_async_copy(via[k], dst[k], sem.at[5 + k]) for k in range(5)]
    for c in into:
        c.start()
    for k in (0, 2, 3, 4, 1):
        into[k].wait()
        out[k].start()
    for c in out:
        c.wait()


def shards(tokens, wp, bp, wi, bi, wo, bo, cot):
    scale = 1.0 / math.sqrt(COLS * TILE_ROWS * NROW)
    table = scratch_table()
    hbm = pl.BlockSpec(memory_space=pl.ANY)
    vmem = pl.BlockSpec(memory_space=pltpu.VMEM)
    share, width = DIM // NCOL, DIM // NROW

    def body(*refs):
        kernel(list(table), scale, *refs)

    shapes = (
        jax.ShapeDtypeStruct((TILE_ROWS, TILE_COLS, DIM), BF),
        jax.ShapeDtypeStruct((TOK, VIT), BF),
        jax.ShapeDtypeStruct((share, VIT // NROW), F32),
        jax.ShapeDtypeStruct((9, share, width), F32),
        jax.ShapeDtypeStruct((9, share, width), F32),
    )
    results = pl.pallas_call(
        body,
        out_shape=shapes,
        in_specs=[hbm, hbm, vmem, hbm, vmem, hbm, vmem, hbm],
        out_specs=(hbm, hbm, vmem, vmem, vmem),
        scratch_shapes=list(table.values()),
        compiler_params=pltpu.CompilerParams(
            collective_id=0, has_side_effects=True, vmem_limit_bytes=60 * 1024 * 1024
        ),
        name="refine_unit",
    )(tokens, wp, bp, wi.reshape(3, WIDE, DIM), bi, wo.reshape(3, WIDE, DIM), bo, cot)
    refined, gtok, gproj, gin, gout = pl.pallas_call(
        hand_over,
        out_shape=shapes,
        in_specs=[hbm] * 5,
        out_specs=(hbm,) * 5,
        scratch_shapes=[pltpu.VMEM(v.shape, v.dtype) for v in shapes] + [pltpu.SemaphoreType.DMA((10,))],
        name="hand_over",
    )(*results)
    turn = lambda g: g.reshape(3, 3, share, width).transpose(0, 1, 3, 2)
    return refined, gtok, gproj.T, turn(gin), turn(gout)


def solution(mesh):
    in_specs = (
        P(("frame", "row", "col"), None),
        P(),
        P(),
        P(),
        P(),
        P(),
        P(),
        P(("frame", "row"), "col", None),
    )
    out_specs = (
        P(("frame", "row"), "col", None),
        P(("frame", "row", "col"), None),
        P(("frame", "row"), "col"),
        P("frame", None, "row", "col"),
        P("frame", None, "row", "col"),
    )
    return jax.shard_map(shards, mesh=mesh, in_specs=in_specs, out_specs=out_specs, check_vma=False)
```

time: 502 us -> 79.4 us (0.16); the launches traced: 493 us -> 79.3 us
  waiting for transfers between devices: 313 us -> 0 us
  Pallas kernels: 0 us -> 78.5 us
  starting transfers between devices: 55.3 us -> 0 us
  local copies, waits for them, and re-layouts: 43 us -> 0 us
  matrix products: 33.7 us -> 0 us
  blocking collectives: 24.2 us -> 0 us
  between operations: 15.8 us -> 0.8 us
  other arithmetic: 8.74 us -> 0 us
    unnamed x11 -> x0, waiting for transfers between devices: 258 us -> none
    pallas_call x0 -> x2, Pallas kernels: none -> 78.5 us  [the longest x1 75.7 us: shards(): pl.pallas_call(body, out_shape=shapes, in_specs=[hbm, hbm, vmem, hbm, vme...]
    reduce_scatter x1 -> x0, waiting for transfers between devices: 48.5 us -> none  [shards(): lax.psum_scatter(row_sums[0].astype(jnp.bfloat16), 'col', scatter_dimensi...]
    ppermute x16 -> x0, starting transfers between devices: 44.8 us -> none  [the longest x8 31.8 us: with_halo(): lax.ppermute(lax.slice_in_dim(block, block.shape[dim] - width, None, axis...]
    unnamed x90 -> x0, local copies, waits for them, and re-layouts: 34.8 us -> none
    dot_general x57 -> x0, matrix products: 33.7 us -> none  [the longest x18 11.2 us: conv_transpose(): jnp.dot(window, kernel[top, left].T, preferred_element_type=jnp.float32)]
    all_to_all x1 -> x0, blocking collectives: 24.2 us -> none  [shards(): lax.all_to_all(back_feature, 'col', split_axis=0, concat_axis=1, tiled=True)]
    all_to_all x1 -> x0, starting transfers between devices: 9.96 us -> none  [shards(): lax.all_to_all(project(strips, project_weight, project_bias), 'col', spli...]
  transfers between devices with their start and end apart: 23 -> 0, of which waited for: 8 -> 0; matrix products, arithmetic and copies ran while one was open for 11% -> 0% of each run, Pallas kernels for 0% -> 0%
where the time goes in v1:
time: 79.4 us; the launch traced here: 79.3 us
  Pallas kernels  78.5 us (99%)
  between operations  0.8 us (1%)
    pallas_call x1, Pallas kernels, shards(): pl.pallas_call(body, out_shape=shapes, in_specs=[hbm, hbm, vmem, hbm, vme...  75.7 us
    pallas_call x1, Pallas kernels, shards(): pl.pallas_call(hand_over, out_shape=shapes, in_specs=[hbm] * 5, out_specs...  2.81 us

profile of v1, /device:TPU:1, one launch (start us, length us, event | category | flops | bytes accessed | tf_op | source)
XLA Modules:
  0.0 79.3 jit_solution(2837751119974142527)
XLA Ops:
  0.6 75.7 %refine_unit.1 = (bf16[32,16,384]{2,1,0:T(8,128)(2,1)}, bf16[512,1536]{1,0:T(8,128)(2,1)}, f32[24,192]{1,0:T(8,128)}, f32[9,24,48]{2,1,0:T(8,128)}, f32[9,24,48]{2,1,0:T(8,128)}) custom-call(bf16[512,1536]{1,0:T(8,128)(2,1)} %refs_0_.1, bf16[1536,384]{1,0:T(8,128)(2,1)} %refs_1_.1, f32[384]{0:T(512)} %refs_2_.1, bf16[3,1152,384]{2,1,0:T(8,128)(2,1)} %bitcast.9, ...), custom_call_target="tpu_custom_call" | custom-call | tf_op jit(solution)/shard_map/refine_unit/pallas_call | solution.py:603
  76.3 2.8 %hand_over.1 = (bf16[32,16,384]{2,1,0:T(8,128)(2,1)}, bf16[512,1536]{1,0:T(8,128)(2,1)}, f32[24,192]{1,0:T(8,128)}, f32[9,24,48]{2,1,0:T(8,128)}, f32[9,24,48]{2,1,0:T(8,128)}) custom-call(bf16[32,16,384]{2,1,0:T(8,128)(2,1)} %get-tuple-element.15.refs_0_, bf16[512,1536]{1,0:T(8,128)(2,1)} %get-tuple-element.16.refs_1_, ...), custom_call_target="tpu_custom_call" | custom-call | tf_op jit(solution)/shard_map/hand_over/pallas_call | solution.py:614

commit v2 on v1

--- a/solution.py
+++ b/solution.py
@@ -52,6 +52,11 @@
         "feat": ((TOK, DIM), BF),
         "bf": ((TOK, DIM), BF),
         "slope": ((TOK, DIM), F32),
+        "acc": ((TOK, DIM), F32),
+        "acc_t": ((TOK, DIM), F32),
+        "bp": ((DIM,), F32),
+        "bi": ((DIM,), F32),
+        "bo": ((DIM,), F32),
         "act_t": ((DIM, TOK), BF),
         "hid_t": ((DIM, TOK), BF),
         "strip": ((2, COLS, DIM), BF),
@@ -82,7 +87,7 @@
         for piece in group:
             out[piece[0] + "_ss"] = pltpu.SemaphoreType.DMA((count,))
             out[piece[0] + "_rs"] = pltpu.SemaphoreType.DMA((count,))
-    out["load"] = pltpu.SemaphoreType.DMA((10,))
+    out["load"] = pltpu.SemaphoreType.DMA((11,))
     out["halo_ss"] = pltpu.SemaphoreType.DMA((8,))
     out["halo_rs"] = pltpu.SemaphoreType.DMA((8,))
     out["swap_ss"] = pltpu.SemaphoreType.DMA((30,))
@@ -334,7 +339,7 @@
 
 
 def kernel(names, scale, *refs):
-    tok_h, wp_h, bp, wi_h, bi, wo_h, bo, cot_h = refs[:8]
+    tok_h, wp_h, bp_h, wi_h, bi_h, wo_h, bo_h, cot_h = refs[:8]
     refined_o, gtok_o, gproj_o, gin_o, gout_o = refs[8:13]
     m = dict(zip(names, refs[13:]))
     w = Where()
@@ -356,12 +361,13 @@
         pl.semaphore_signal(barrier, inc=1, device_id=device, device_id_type=MESH)
 
     load = m["load"]
-    loads = [
-        pltpu.make_async_copy(src, m[dst], load.at[k])
-        for k, (src, dst) in enumerate(((tok_h, "tok"), (wp_h, "wp"), (wi_h, "wi"), (wo_h, "wo")))
-    ]
-    loads[0].start()
-    loads[1].start()
+    sources = {"tok": tok_h, "wp": wp_h, "bp": bp_h, "wi": wi_h, "bi": bi_h, "wo": wo_h, "bo": bo_h}
+    loads = {
+        name: pltpu.make_async_copy(src, m[name], load.at[k])
+        for k, (name, src) in enumerate(sources.items())
+    }
+    for name in ("tok", "wp", "bp", "bi", "bo"):
+        loads[name].start()
     here = pl.ds(pl.multiple_of(w.c * TILE_COLS, TILE_COLS), TILE_COLS)
     mine = pl.ds(w.c * 2, 2)
     cot = m["cot"]
@@ -397,19 +403,37 @@
         copies[1].wait_recv()
         expand(center, wide, 3, flip)
 
-    def conv(wide, kern):
-        total = dot(wide[0:TOK], kern[0])
-        total = total + dot(wide[COLS : COLS + TOK], kern[1])
-        return total + dot(wide[2 * COLS : 2 * COLS + TOK], kern[2])
-
-    def conv_t(wide, kern):
-        total = jnp.zeros((TOK, DIM), F32)
-        for a in range(3):
-            at = slice((2 - a) * COLS, (2 - a) * COLS + TOK)
-            for b in range(3):
-                lanes = slice(b * DIM, (b + 1) * DIM)
-                total = total + dot_nt(wide[at, lanes], kern[a, lanes])
+    acc, acc_t = m["acc"], m["acc_t"]
+    first, second = slice(0, COLS), slice(COLS, TOK)
+
+    def row(wide, k):
+        return wide[k * COLS : (k + 1) * COLS]
+
+    def conv_inner(wide, kern):
+        acc[...] = dot(wide[COLS : 3 * COLS], kern[1])
+        acc[first] += dot(row(wide, 2), kern[2])
+        acc[second] += dot(row(wide, 1), kern[0])
+
+    def conv_rim(wide, kern):
+        acc[first] += dot(row(wide, 0), kern[0])
+        acc[second] += dot(row(wide, 3), kern[2])
+
+    def taps_t(wide, k0, k1, kern, a):
+        total = None
+        for b in range(3):
+            lanes = slice(b * DIM, (b + 1) * DIM)
+            term = dot_nt(wide[k0 * COLS : k1 * COLS, lanes], kern[a, lanes])
+            total = term if total is None else total + term
         return total
+
+    def conv_t_inner(wide, kern):
+        acc_t[...] = taps_t(wide, 1, 3, kern, 1)
+        acc_t[first] += taps_t(wide, 2, 3, kern, 0)
+        acc_t[second] += taps_t(wide, 1, 2, kern, 2)
+
+    def conv_t_rim(wide, kern):
+        acc_t[first] += taps_t(wide, 0, 1, kern, 2)
+        acc_t[second] += taps_t(wide, 3, 4, kern, 0)
 
     def weight_grad(left_t, wide, name):
         for a in sorted({t // 3 for t in taps[name]}):
@@ -420,22 +444,10 @@
                     g[:, b * DIM : (b + 1) * DIM].astype(BF).reshape(NROW, width, DIM)
                 )
 
-    act, hid, bh = m["act"], m["hid"], m["bh"]
-    loads[0].wait()
-    loads[1].wait()
-    loads[2].start()
-    own_cot = pltpu.make_async_copy(cot_h.at[mine], cot.at[pl.ds(1, 2), here], load.at[4])
-    own_cot.start()
-    feature = (dot(m["tok"][...], m["wp"][...]) + bp[...][None, :]).astype(BF)
-    m["feat"][...] = feature
-    activated = silu(feature.astype(F32)).astype(BF)
-    act[1:3] = activated.reshape(2, COLS, DIM)
-
     pl.semaphore_wait(barrier, len(friends))
-
-    act_halo = halo(act, 0)
+    turn = [8, 7, 9, 6, 10, 5, 11, 4, 12, 3, 13, 2, 14, 1, 15]
     cot_copies = []
-    for k in range(1, NCOL):
+    for k in turn:
         there = (w.c + k) % NCOL
         cot_copies.append(
             remote(
@@ -447,24 +459,27 @@
             )
         )
         cot_copies[-1].start()
-    loads[3].start()
+    own_cot = pltpu.make_async_copy(cot_h.at[mine], cot.at[pl.ds(1, 2), here], load.at[7])
+    own_cot.start()
+
+    act, hid, bh = m["act"], m["hid"], m["bh"]
+    for name in ("tok", "wp", "bp"):
+        loads[name].wait()
+    loads["wi"].start()
+    feature = (dot(m["tok"][...], m["wp"][...]) + m["bp"][...][None, :]).astype(BF)
+    m["feat"][...] = feature
+    act[1:3] = silu(feature.astype(F32)).astype(BF).reshape(2, COLS, DIM)
+    act_halo = halo(act, 0)
+    loads["wo"].start()
     for z in (zo, zi, zp):
         z.clear()
-    m["act_t"][...] = act[1:3].reshape(TOK, DIM).T
     expand(act, m["ea"], 1, False)
     expand(act, m["ea"], 2, False)
+
+    loads["wi"].wait()
+    conv_inner(m["ea"], m["wi"])
+    m["act_t"][...] = act[1:3].reshape(TOK, DIM).T
     m["tok_t"][...] = m["tok"][...].T
-    expand_rim(act, m["ea"], act_halo, False)
-
-    loads[2].wait()
-    pre = conv(m["ea"], m["wi"]) + bi[...][None, :]
-    hidden = silu(pre).astype(BF)
-    m["slope"][...] = silu_slope(pre)
-    hid[1:3] = hidden.reshape(2, COLS, DIM)
-    hid_halo = halo(hid, 2)
-    m["hid_t"][...] = hid[1:3].reshape(TOK, DIM).T
-    expand(hid, m["eh"], 1, False)
-    expand(hid, m["eh"], 2, False)
 
     own_cot.wait()
     for c in cot_copies:
@@ -472,31 +487,59 @@
     cot_halo = halo(cot, 4)
     expand(cot, m["ec"], 1, True)
     expand(cot, m["ec"], 2, True)
+    loads["wo"].wait()
+    conv_t_inner(m["ec"], m["wo"])
+    expand_rim(act, m["ea"], act_halo, False)
+    conv_rim(m["ea"], m["wi"])
+    loads["bi"].wait()
+    pre = acc[...] + m["bi"][...][None, :]
+    hid[1:3] = silu(pre).astype(BF).reshape(2, COLS, DIM)
+    m["slope"][...] = silu_slope(pre)
+    m["hid_t"][...] = hid[1:3].reshape(TOK, DIM).T
     weight_grad(m["hid_t"], m["ec"], "o1")
     o1.stage0()
-    expand_rim(hid, m["eh"], hid_halo, False)
-    loads[3].wait()
-    refined = m["feat"][...].astype(F32) + conv(m["eh"], m["wo"]) + bo[...][None, :]
-    m["strip"][...] = refined.astype(BF).reshape(2, COLS, DIM)
-    o1.stage1()
     expand_rim(cot, m["ec"], cot_halo, True)
 
-    bh[1:3] = (conv_t(m["ec"], m["wo"]) * m["slope"][...]).astype(BF).reshape(2, COLS, DIM)
+    conv_t_rim(m["ec"], m["wo"])
+    bh[1:3] = (acc_t[...] * m["slope"][...]).astype(BF).reshape(2, COLS, DIM)
     bh_halo = halo(bh, 6)
     weight_grad(m["hid_t"], m["ec"], "o2")
     o2.stage0()
+    o1.stage1()
     expand(bh, m["ea"], 1, True)
     expand(bh, m["ea"], 2, True)
     weight_grad(m["act_t"], m["ea"], "i1")
     i1.stage0()
-    o1.stage2()
+    conv_t_inner(m["ea"], m["wi"])
     o2.stage1()
     expand_rim(bh, m["ea"], bh_halo, True)
-
-    own_refined = pltpu.make_async_copy(m["strip"].at[:, here], m["tile"].at[mine], load.at[5])
-    own_refined.start()
+    hid_halo = halo(hid, 2)
+
+    weight_grad(m["act_t"], m["ea"], "i2")
+    i2.stage0()
+    i1.stage1()
+    conv_t_rim(m["ea"], m["wi"])
+    back = acc_t[...] * silu_slope(m["feat"][...].astype(F32))
+    m["bf"][...] = (cot[1:3].reshape(TOK, DIM).astype(F32) + back).astype(BF)
+    o1.stage2()
+    pp.part[...] = dot(m["tok_t"][...], m["bf"][...]).astype(BF).reshape(NROW, VIT // NROW, DIM)
+    pp.stage0()
+    i2.stage1()
+    o2.stage2()
+    pp.stage1()
+    o1.stage3()
+
+    expand(hid, m["eh"], 1, False)
+    expand(hid, m["eh"], 2, False)
+    conv_inner(m["eh"], m["wo"])
+    o1.stage4()
+    expand_rim(hid, m["eh"], hid_halo, False)
+    conv_rim(m["eh"], m["wo"])
+    loads["bo"].wait()
+    refined = m["feat"][...].astype(F32) + acc[...] + m["bo"][...][None, :]
+    m["strip"][...] = refined.astype(BF).reshape(2, COLS, DIM)
     refined_copies = []
-    for k in range(1, NCOL):
+    for k in turn:
         there = (w.c + k) % NCOL
         refined_copies.append(
             remote(
@@ -508,29 +551,17 @@
             )
         )
         refined_copies[-1].start()
-
-    i1.stage1()
-    weight_grad(m["act_t"], m["ea"], "i2")
-    i2.stage0()
-    o1.stage3()
-    back = conv_t(m["ea"], m["wi"]) * silu_slope(m["feat"][...].astype(F32))
-    back_feature = (cot[1:3].reshape(TOK, DIM).astype(F32) + back).astype(BF)
-    m["bf"][...] = back_feature
-    o2.stage2()
-    i2.stage1()
-    pp.part[...] = dot(m["tok_t"][...], m["bf"][...]).astype(BF).reshape(NROW, VIT // NROW, DIM)
-    pp.stage0()
+    own_refined = pltpu.make_async_copy(m["strip"].at[:, here], m["tile"].at[mine], load.at[8])
+    own_refined.start()
     i1.stage2()
-    o1.stage4()
     o2.stage3()
-    pp.stage1()
+    m["gtok"][...] = dot_nt(m["bf"][...], m["wp"][...]).astype(BF)
+    gtok_copy = pltpu.make_async_copy(m["gtok"], gtok_o, load.at[9])
+    gtok_copy.start()
     i1.stage3()
-    m["gtok"][...] = dot_nt(m["bf"][...], m["wp"][...]).astype(BF)
-    gtok_copy = pltpu.make_async_copy(m["gtok"], gtok_o, load.at[6])
-    gtok_copy.start()
+    i2.stage2()
     o2.stage4()
     zo.stage4()
-    i2.stage2()
     i1.stage4()
     pp.stage2()
     i2.stage3()
@@ -543,7 +574,7 @@
     own_refined.wait()
     for c in refined_copies:
         c.wait_recv()
-    refined_copy = pltpu.make_async_copy(m["tile"], refined_o, load.at[7])
+    refined_copy = pltpu.make_async_copy(m["tile"], refined_o, load.at[10])
     refined_copy.start()
     zi.stage5()
     zp.stage5()
@@ -572,11 +603,15 @@
 
 def hand_over(*refs):
     src, dst, via, sem = refs[:5], refs[5:10], refs[10:15], refs[15]
-    into = [pltpu.make_async_copy(src[k], via[k], sem.at[k]) for k in range(5)]
-    out = [pltpu.make_async_copy(via[k], dst[k], sem.at[5 + k]) for k in range(5)]
+    part = TOK // 4
+    views = [[ref.at[pl.ds(j * part, part)] for j in range(4)] for ref in (src[1], via[1], dst[1])]
+    for k, group in enumerate((src, via, dst)):
+        views[k] += [group[j] for j in (0, 2, 3, 4)]
+    into = [pltpu.make_async_copy(views[0][k], views[1][k], sem.at[k]) for k in range(8)]
+    out = [pltpu.make_async_copy(views[1][k], views[2][k], sem.at[8 + k]) for k in range(8)]
     for c in into:
         c.start()
-    for k in (0, 2, 3, 4, 1):
+    for k in range(8):
         into[k].wait()
         out[k].start()
     for c in out:
@@ -603,7 +638,7 @@
     results = pl.pallas_call(
         body,
         out_shape=shapes,
-        in_specs=[hbm, hbm, vmem, hbm, vmem, hbm, vmem, hbm],
+        in_specs=[hbm] * 8,
         out_specs=(hbm, hbm, vmem, vmem, vmem),
         scratch_shapes=list(table.values()),
         compiler_params=pltpu.CompilerParams(
@@ -616,7 +651,7 @@
         out_shape=shapes,
         in_specs=[hbm] * 5,
         out_specs=(hbm,) * 5,
-        scratch_shapes=[pltpu.VMEM(v.shape, v.dtype) for v in shapes] + [pltpu.SemaphoreType.DMA((10,))],
+        scratch_shapes=[pltpu.VMEM(v.shape, v.dtype) for v in shapes] + [pltpu.SemaphoreType.DMA((16,))],
         name="hand_over",
     )(*results)
     turn = lambda g: g.reshape(3, 3, share, width).transpose(0, 1, 3, 2)

time: 79.4 us -> 73.1 us (0.921)
  Pallas kernels: 78.5 us -> 71.7 us
    pallas_call x1, Pallas kernels: 75.7 us -> 69.2 us  [shards(): pl.pallas_call(body, out_shape=shapes, in_specs=[hbm] * 8, out_specs=(hbm...]
where the time goes in v2:
time: 73.1 us; the launch traced here: 72.5 us
  Pallas kernels  71.7 us (98%)
  between operations  0.8 us (1%)
    pallas_call x1, Pallas kernels, shards(): pl.pallas_call(body, out_shape=shapes, in_specs=[hbm] * 8, out_specs=(hbm...  69.2 us
    pallas_call x1, Pallas kernels, shards(): pl.pallas_call(hand_over, out_shape=shapes, in_specs=[hbm] * 5, out_specs...  2.47 us

profile of v2, /device:TPU:1, one launch (start us, length us, event | category | flops | bytes accessed | tf_op | source)
XLA Modules:
  0.0 72.5 jit_solution(7079881879692746908)
XLA Ops:
  0.6 69.2 %refine_unit.1 = (bf16[32,16,384]{2,1,0:T(8,128)(2,1)}, bf16[512,1536]{1,0:T(8,128)(2,1)}, f32[24,192]{1,0:T(8,128)}, f32[9,24,48]{2,1,0:T(8,128)}, f32[9,24,48]{2,1,0:T(8,128)}) custom-call(bf16[512,1536]{1,0:T(8,128)(2,1)} %refs_0_.1, bf16[1536,384]{1,0:T(8,128)(2,1)} %refs_1_.1, f32[384]{0:T(512)} %refs_2_.1, bf16[3,1152,384]{2,1,0:T(8,128)(2,1)} %bitcast.9, ...), custom_call_target="tpu_custom_call" | custom-call | tf_op jit(solution)/shard_map/refine_unit/pallas_call | solution.py:638
  69.8 2.5 %hand_over.1 = (bf16[32,16,384]{2,1,0:T(8,128)(2,1)}, bf16[512,1536]{1,0:T(8,128)(2,1)}, f32[24,192]{1,0:T(8,128)}, f32[9,24,48]{2,1,0:T(8,128)}, f32[9,24,48]{2,1,0:T(8,128)}) custom-call(bf16[32,16,384]{2,1,0:T(8,128)(2,1)} %get-tuple-element.15.refs_0_, bf16[512,1536]{1,0:T(8,128)(2,1)} %get-tuple-element.16.refs_1_, ...), custom_call_target="tpu_custom_call" | custom-call | tf_op jit(solution)/shard_map/hand_over/pallas_call | solution.py:649

commit v3 on v2

--- a/solution.py
+++ b/solution.py
@@ -499,13 +499,13 @@
     weight_grad(m["hid_t"], m["ec"], "o1")
     o1.stage0()
     expand_rim(cot, m["ec"], cot_halo, True)
+    o1.stage1()
 
     conv_t_rim(m["ec"], m["wo"])
     bh[1:3] = (acc_t[...] * m["slope"][...]).astype(BF).reshape(2, COLS, DIM)
     bh_halo = halo(bh, 6)
     weight_grad(m["hid_t"], m["ec"], "o2")
     o2.stage0()
-    o1.stage1()
     expand(bh, m["ea"], 1, True)
     expand(bh, m["ea"], 2, True)
     weight_grad(m["act_t"], m["ea"], "i1")
@@ -518,14 +518,14 @@
     weight_grad(m["act_t"], m["ea"], "i2")
     i2.stage0()
     i1.stage1()
+    o1.stage2()
     conv_t_rim(m["ea"], m["wi"])
     back = acc_t[...] * silu_slope(m["feat"][...].astype(F32))
     m["bf"][...] = (cot[1:3].reshape(TOK, DIM).astype(F32) + back).astype(BF)
-    o1.stage2()
     pp.part[...] = dot(m["tok_t"][...], m["bf"][...]).astype(BF).reshape(NROW, VIT // NROW, DIM)
     pp.stage0()
+    o2.stage2()
     i2.stage1()
-    o2.stage2()
     pp.stage1()
     o1.stage3()
 

time: 73.1 us -> 73.5 us (level)
  Pallas kernels: 71.7 us -> 72.5 us
    pallas_call x1, Pallas kernels: 69.2 us -> 70.1 us  [shards(): pl.pallas_call(body, out_shape=shapes, in_specs=[hbm] * 8, out_specs=(hbm...]
where the time goes in v3:
time: 73.5 us; the launch traced here: 73.3 us
  Pallas kernels  72.5 us (99%)
  between operations  0.8 us (1%)
    pallas_call x1, Pallas kernels, shards(): pl.pallas_call(body, out_shape=shapes, in_specs=[hbm] * 8, out_specs=(hbm...  70.1 us
    pallas_call x1, Pallas kernels, shards(): pl.pallas_call(hand_over, out_shape=shapes, in_specs=[hbm] * 5, out_specs...  2.47 us

profile of v3, /device:TPU:1, one launch (start us, length us, event | category | flops | bytes accessed | tf_op | source)
XLA Modules:
  0.0 73.3 jit_solution(6261026690081435279)
XLA Ops:
  0.6 70.1 %refine_unit.1 = (bf16[32,16,384]{2,1,0:T(8,128)(2,1)}, bf16[512,1536]{1,0:T(8,128)(2,1)}, f32[24,192]{1,0:T(8,128)}, f32[9,24,48]{2,1,0:T(8,128)}, f32[9,24,48]{2,1,0:T(8,128)}) custom-call(bf16[512,1536]{1,0:T(8,128)(2,1)} %refs_0_.1, bf16[1536,384]{1,0:T(8,128)(2,1)} %refs_1_.1, f32[384]{0:T(512)} %refs_2_.1, bf16[3,1152,384]{2,1,0:T(8,128)(2,1)} %bitcast.9, ...), custom_call_target="tpu_custom_call" | custom-call | tf_op jit(solution)/shard_map/refine_unit/pallas_call | solution.py:638
  70.7 2.5 %hand_over.1 = (bf16[32,16,384]{2,1,0:T(8,128)(2,1)}, bf16[512,1536]{1,0:T(8,128)(2,1)}, f32[24,192]{1,0:T(8,128)}, f32[9,24,48]{2,1,0:T(8,128)}, f32[9,24,48]{2,1,0:T(8,128)}) custom-call(bf16[32,16,384]{2,1,0:T(8,128)(2,1)} %get-tuple-element.15.refs_0_, bf16[512,1536]{1,0:T(8,128)(2,1)} %get-tuple-element.16.refs_1_, ...), custom_call_target="tpu_custom_call" | custom-call | tf_op jit(solution)/shard_map/hand_over/pallas_call | solution.py:649
